TPU v7x, 128 devices: a whole 4x4x4 slice. The times are simulated.
128 devices in a mesh: seq: 32 (over y, x, core), batch: 4 (over z).
Axes of the slice: x: 4, y: 4, z: 4, core: 2. Of those that a mesh axis runs over, the one named last changes fastest.
Arguments:
- tokens: bfloat16 [4, 16384, 768], P('batch', 'seq'), may hold values from -6 to 6
- lengths: int32 [4], P('batch'), may hold values from 8192 to 16384, as said below
- w_query: bfloat16 [768, 768], replicated, may hold values from -0.21875 to 0.21875
- b_query: float32 [768], replicated, may hold values from -3 to 3
- w_key: bfloat16 [768, 768], replicated, may hold values from -0.21875 to 0.21875
- b_key: float32 [768], replicated, may hold values from -3 to 3
- w_value: bfloat16 [768, 768], replicated, may hold values from -0.21875 to 0.21875
- b_value: float32 [768], replicated, may hold values from -0.3125 to 0.3125
- w_out: bfloat16 [768, 768], replicated, may hold values from -3 to 3
- b_out: float32 [768], replicated, may hold values from -1.75 to 1.75
- gain_one: float32 [768], replicated, may hold values from 0.1 to 1.9
- shift_one: float32 [768], replicated, may hold values from -1.75 to 1.75
- w_up: bfloat16 [768, 3072], replicated, may hold values from -0.21875 to 0.21875
- b_up: float32 [3072], replicated, may hold values from -1.75 to 1.75
- w_down: bfloat16 [3072, 768], replicated, may hold values from -0.109375 to 0.109375
- b_down: float32 [768], replicated, may hold values from -1.75 to 1.75
- gain_two: float32 [768], replicated, may hold values from 0.1 to 1.9
- shift_two: float32 [768], replicated, may hold values from -1.75 to 1.75
- cotangent: bfloat16 [4, 16384, 768], P('batch', 'seq'), may hold values from -6 to 6
Outputs:
- block_out: bfloat16 [4, 16384, 768], P('batch', 'seq')
- grad_tokens: float32 [4, 16384, 768], P('batch', 'seq')
- grad_w_query: float32 [768, 768], P('seq')
- grad_b_query: float32 [768], P('seq')
- grad_w_key: float32 [768, 768], P('seq')
- grad_b_key: float32 [768], P('seq')
- grad_w_value: float32 [768, 768], P('seq')
- grad_b_value: float32 [768], P('seq')
- grad_w_out: float32 [768, 768], P('seq')
- grad_b_out: float32 [768], P('seq')
- grad_gain_one: float32 [768], P('seq')
- grad_shift_one: float32 [768], P('seq')
- grad_w_up: float32 [768, 3072], P('seq')
- grad_b_up: float32 [3072], P('seq')
- grad_w_down: float32 [3072, 768], P('seq')
- grad_b_down: float32 [768], P('seq')
- grad_gain_two: float32 [768], P('seq')
- grad_shift_two: float32 [768], P('seq')
Inputs may be any that keep to these rules, and one draw needn't show every extreme that they name: `lengths`: in every draw one sequence has all 16384 positions real and another has exactly 8192.
All inputs are finite; a program needn't handle non-finite values.
Results may differ from a plain program's by a relative error of at most 0.012.
Values sent between devices are 32-bit elements; how exact they have to be, the bound alone decides.
A program may use at most 192 MiB of HBM per device.

v0:
```python
import jax
import jax.numpy as jnp
from jax import lax
from jax.experimental import pallas as pl
from jax.experimental.pallas import tpu as pltpu
from jax.sharding import Mesh
from jax.sharding import PartitionSpec as P

SEQ = ("seq_0", "seq_1", "seq_2")
AX = ("seq_0", "seq_1", "batch")
CORE = "seq_2"
MESH = pl.DeviceIdType.MESH
DIRECT = (1, 3, 2)
F32 = jnp.float32
BF16 = jnp.bfloat16
HALF_PI = 1.5707963267948966
HALF_PI_REST = -4.371139000186241e-08
EPSILON = 1e-05
ROWS = 512
WIDTH = 768
HIDDEN = 3072
HEADS = 12
PAIRS = 6
CHUNK = 256
FEED = 1024
TILE = 1536
VMEM = pltpu.VMEM
LIMIT = 63 * 2**20


def loop(count, body, after=None):
    def step(k, carry):
        with jax.named_scope(body.__name__):
            body(k)
        for n, then in (after or {}).items():
            pl.when(k == n)(then)

    lax.fori_loop(0, count, step, None)


def each_of(count, body):
    lax.fori_loop(0, count, lambda k, carry: body(k), None)


def nn(a, b):
    return jnp.dot(a, b, preferred_element_type=F32)


def nt(a, b):
    return lax.dot_general(a, b, (((1,), (1,)), ((), ())), preferred_element_type=F32)


def tn(a, b):
    return lax.dot_general(a, b, (((0,), (0,)), ((), ())), preferred_element_type=F32)


def at(k, size):
    return pl.ds(pl.multiple_of(k * size, size), size)


def rot(k, d):
    return lax.rem(k + d, 4)


def left_lanes(rows):
    return lax.broadcasted_iota(jnp.int32, (rows, 128), 1) < 64


def swap_halves(value):
    return pltpu.roll(value, 64, 1)


def doubled(value):
    return jnp.concatenate([value, value], axis=1)


def halves(value):
    high = value.astype(BF16)
    return high, (value - high.astype(F32)).astype(BF16)


SIN = (1.0, -0.1666666716337204, 0.008333330973982811, -0.00019840864115394652, 2.7525297809916083e-06, -2.3888299338636898e-08)


def sine(x):
    square = x * x
    value = SIN[5]
    for c in SIN[4::-1]:
        value = value * square + c
    return value * x


def normal_parts(p):
    return 0.5 + 0.5 * lax.erf(p * 0.7071067811865476), 0.3989422804014327 * jnp.exp(-0.5 * p * p)


def trig_block(first, rows, length):
    position = first + lax.broadcasted_iota(jnp.int32, (rows, 128), 0)
    size = lax.broadcast_in_dim(length, (rows, 128), ()).astype(F32)
    angle = HALF_PI * jnp.minimum(position + 1, length).astype(F32) / size
    both = sine(jnp.where(left_lanes(rows), (HALF_PI - angle) + HALF_PI_REST, angle))
    return both, (position < length).astype(F32)


def project_values(n, x_ref, w, b, out):
    left = left_lanes(ROWS)
    u = (nn(x_ref[...], w[:, at(n, 256)]) + b[:, at(n, 256)]).astype(BF16).astype(F32)
    for j in range(2):
        part = u[:, 128 * j : 128 * j + 128]
        out[:, at(4 * n + 2 * j, 128)] = jnp.where(left, part, 1.0).astype(BF16)
        out[:, at(4 * n + 2 * j + 1, 128)] = jnp.where(left, swap_halves(part), 1.0).astype(BF16)


def project_soft(n, x_ref, w, b, table, out, first, gates, gate):
    left = left_lanes(ROWS)
    u = nn(x_ref[...], w[:, at(n, 256)]) + b[:, at(n, 256)]
    small = jnp.exp(-jnp.abs(u))
    soft = jnp.maximum(u, 0.0) + jnp.log1p(small)
    gates[:, at(gate + n, 256)] = (0.5 + 0.5 * jnp.tanh(0.5 * u)).astype(BF16)
    trig = table[...]
    for j in range(2):
        part = soft[:, 128 * j : 128 * j + 128]
        other = swap_halves(part)
        out[:, at(first + 4 * n + 2 * j, 128)] = (jnp.where(left, part, other) * trig).astype(BF16)
        out[:, at(first + 4 * n + 2 * j + 1, 128)] = (jnp.where(left, other, part) * trig).astype(BF16)


def state_sums(p, qk_ref, v_ref, state_ref, early_ref):
    for j in range(2):
        h = 2 * p + j
        keys, values = at(HEADS + h, 128), at(h, 128)
        early = tn(v_ref[0:CHUNK, values], qk_ref[0:CHUNK, keys])
        early_ref[h] = early[0:72]
        both = early + tn(v_ref[CHUNK:ROWS, values], qk_ref[CHUNK:ROWS, keys])
        state_ref[p, 64 * j : 64 * j + 64] = both[0:64]
        state_ref[p, 128 + j : 129 + j] = both[64:65]
    state_ref[p, 130:136] = jnp.zeros((6, 128), F32)


def exchange_steps(n, pay, out, core_in, chip, head, tail, total, msgs, xa, ya, yb, xb, send, recv):
    my, mx = lax.axis_index("seq_0"), lax.axis_index("seq_1")
    core = lax.axis_index(CORE)
    other = 1 - core
    own = 2 * n + core

    def remote(src, dst, stage, k, target):
        pltpu.make_async_remote_copy(
            src_ref=src, dst_ref=dst, send_sem=send.at[n, stage], recv_sem=recv.at[n, k],
            device_id=target, device_id_type=MESH).start()

    def counts(theirs, mine):
        return theirs < mine

    def chosen(flag, value):
        return jnp.where(flag, value, jnp.zeros_like(value))

    def first():
        remote(pay.at[2 * n + other], core_in.at[n], 0, 0, {CORE: other})

    def second():
        arrived(core_in.at[n], recv.at[n, 0])
        chip[n] = pay[own] + core_in[n]
        for k, d in enumerate(DIRECT):
            remote(chip.at[n, pl.ds(0, 72)], xa.at[n, k], 1, 1, {"seq_1": rot(mx, d)})
        for k, d in enumerate(DIRECT):
            remote(chip.at[n, pl.ds(72, 64)], yb.at[n, k], 1, 2, {"seq_0": rot(my, d)})

    def third():
        arrived(xa.at[n], recv.at[n, 1])
        some, every = jnp.zeros((72, 128), F32), chip[n, 0:72]
        for k, d in enumerate(DIRECT):
            some = some + chosen(counts(rot(mx, 4 - d), mx), xa[n, k])
            every = every + xa[n, k]
        head[n] = some
        total[n] = every
        for k, d in enumerate(DIRECT):
            remote(total.at[n], ya.at[n, k], 2, 3, {"seq_0": rot(my, d)})
        arrived(yb.at[n], recv.at[n, 2])
        some = jnp.zeros((64, 128), F32)
        for k, d in enumerate(DIRECT):
            some = some + chosen(counts(rot(my, 4 - d), my), yb[n, k])
        tail[n] = some
        for k, d in enumerate(DIRECT):
            msgs[n, k] = some + chosen(counts(mx, rot(mx, d)), chip[n, 72:136])
        for k, d in enumerate(DIRECT):
            remote(msgs.at[n, k], xb.at[n, k], 2, 4, {"seq_1": rot(mx, d)})

    def fourth():
        arrived(ya.at[n], recv.at[n, 3])
        arrived(xb.at[n], recv.at[n, 4])
        arrived(chip, send.at[n, 1])
        mine = core == 1
        low, high = head[n], tail[n]
        for k, d in enumerate(DIRECT):
            low = low + chosen(counts(rot(my, 4 - d), my), ya[n, k])
            high = high + xb[n, k]
        out[own, 0:72] = low + chosen(mine, core_in[n, 0:72])
        out[own, 72:136] = high + chosen(mine, core_in[n, 72:136])
        chip[n, 0:72] = low + chosen(jnp.logical_not(mine), pay[own, 0:72])
        chip[n, 72:136] = high + chosen(jnp.logical_not(mine), pay[own, 72:136])
        remote(chip.at[n], out.at[own], 3, 5, {CORE: other})

    def fifth():
        arrived(out.at[2 * n + other], recv.at[n, 5])

    def sent():
        arrived(core_in.at[n], send.at[n, 0])
        arrived(chip, send.at[n, 2])
        arrived(chip.at[n], send.at[n, 3])

    return first, second, third, fourth, fifth, sent


EXCHANGE_SCRATCH = [
    VMEM((3, 136, 128), F32),
    VMEM((3, 136, 128), F32),
    VMEM((3, 72, 128), F32),
    VMEM((3, 64, 128), F32),
    VMEM((3, 72, 128), F32),
    VMEM((3, 3, 64, 128), F32),
    VMEM((3, 3, 72, 128), F32),
    VMEM((3, 3, 72, 128), F32),
    VMEM((3, 3, 64, 128), F32),
    VMEM((3, 3, 64, 128), F32),
    pltpu.SemaphoreType.DMA((3, 4)),
    pltpu.SemaphoreType.DMA((3, 6)),
]


def quarter_steps(n, pay, out, core_in, chip, xa, total, ya, msgs, got, send, recv):
    my, mx = lax.axis_index("seq_0"), lax.axis_index("seq_1")
    core = lax.axis_index(CORE)
    other = 1 - core
    own = 2 * n + core

    def remote(src, dst, stage, k, target):
        pltpu.make_async_remote_copy(
            src_ref=src, dst_ref=dst, send_sem=send.at[n, stage], recv_sem=recv.at[n, k],
            device_id=target, device_id_type=MESH).start()

    def chosen(flag, value):
        return jnp.where(flag, value, jnp.zeros_like(value))

    def first():
        remote(pay.at[2 * n + other], core_in.at[n], 0, 0, {CORE: other})

    def second():
        arrived(core_in.at[n], recv.at[n, 0])
        chip[n] = pay[own] + core_in[n]
        for k, d in enumerate(DIRECT):
            remote(chip.at[n, rot(mx, d)], xa.at[n, k], 1, 1, {"seq_1": rot(mx, d)})

    def third():
        arrived(xa.at[n], recv.at[n, 1])
        total[n] = chip[n, mx] + xa[n, 0] + xa[n, 1] + xa[n, 2]
        for k, d in enumerate(DIRECT):
            remote(total.at[n], ya.at[n, k], 2, 2, {"seq_0": rot(my, d)})

    def cross():
        arrived(ya.at[n], recv.at[n, 2])
        behind = jnp.zeros((40, 128), F32)
        for k, d in enumerate(DIRECT):
            behind = behind + chosen(rot(my, 4 - d) > my, ya[n, k])

        def for_column(column):
            value = behind + chosen(mx > column, chip[n, mx])
            for k, d in enumerate(DIRECT):
                value = value + chosen(rot(mx, 4 - d) > column, xa[n, k])
            return value

        for k, d in enumerate(DIRECT):
            msgs[n, k] = for_column(rot(mx, d))
            remote(msgs.at[n, k], got.at[n, mx], 3, 3, {"seq_1": rot(mx, d)})
        got[n, mx] = for_column(mx)

    def fourth():
        arrived(xa.at[n], recv.at[n, 3])
        arrived(xa.at[n], send.at[n, 1])
        out[own] = got[n] + chosen(core == 0, core_in[n])
        chip[n] = got[n] + chosen(core == 1, pay[own])
        remote(chip.at[n], out.at[own], 4, 4, {CORE: other})

    def fifth():
        arrived(out.at[2 * n + other], recv.at[n, 4])

    def sent():
        arrived(chip.at[n], send.at[n, 0])
        arrived(xa.at[n], send.at[n, 2])
        arrived(xa.at[n], send.at[n, 3])
        arrived(chip.at[n], send.at[n, 4])

    return first, second, third, fourth, fifth, sent, cross


QUARTER_SCRATCH = [
    VMEM((3, 4, 40, 128), F32),
    VMEM((3, 4, 40, 128), F32),
    VMEM((3, 3, 40, 128), F32),
    VMEM((3, 40, 128), F32),
    VMEM((3, 3, 40, 128), F32),
    VMEM((3, 3, 40, 128), F32),
    VMEM((3, 4, 40, 128), F32),
    pltpu.SemaphoreType.DMA((3, 5)),
    pltpu.SemaphoreType.DMA((3, 5)),
]


class Exchange:
    def __init__(self, steps, *refs):
        self.steps = lambda n: steps(n, *refs)

    def step(self, k, n):
        with jax.named_scope(("swap", "begin", "turn", "end", "share", "sent", "cross")[k]):
            self.steps(n)[k]()


def greet(axes):
    barrier = pltpu.get_barrier_semaphore()
    core = lax.axis_index(CORE)
    pl.semaphore_signal(barrier, inc=1, device_id={CORE: 1 - core}, device_id_type=MESH)
    for axis in axes:
        mine = lax.axis_index(axis)
        for d in DIRECT:
            pl.semaphore_signal(barrier, inc=1, device_id={axis: rot(mine, d)}, device_id_type=MESH)


def greeted(axes):
    pl.semaphore_wait(pltpu.get_barrier_semaphore(), 1 + 3 * len(axes))


def causal_masks():
    row = lax.broadcasted_iota(jnp.int32, (CHUNK, CHUNK), 0)
    col = lax.broadcasted_iota(jnp.int32, (CHUNK, CHUNK), 1)
    return row >= col, row <= col


def prefix_state(before, p, j, early_ref, c):
    body, row = before[p, 64 * j : 64 * j + 64], before[p, 128 + j : 129 + j]
    if c == 1:
        body, row = body + early_ref[2 * p + j, 0:64], row + early_ref[2 * p + j, 64:65]
    return jnp.concatenate([body, jnp.broadcast_to(row, (64, 128))], axis=0)


def attend_local(p, qk_ref, v_ref, top_ref, under_ref):
    causal, _ = causal_masks()
    left = left_lanes(CHUNK)
    cols = at(p, 128)
    for c in range(2):
        rows = slice(CHUNK * c, CHUNK * c + CHUNK)
        sums = []
        for j in range(2):
            h = 2 * p + j
            weight = nt(qk_ref[rows, at(h, 128)], qk_ref[rows, at(HEADS + h, 128)])
            sums.append(nn(jnp.where(causal, weight, 0.0).astype(BF16), v_ref[rows, at(h, 128)]))
        even, odd = sums
        top_ref[rows, cols] = jnp.where(left, even, swap_halves(odd))
        under_ref[rows, cols] = jnp.where(left, swap_halves(even), odd)


def attend_earlier(p, qk_ref, early_ref, before, ratio_ref, inverse_ref, mixed_ref):
    left = left_lanes(CHUNK)
    cols = at(p, 128)
    for c in range(2):
        rows = slice(CHUNK * c, CHUNK * c + CHUNK)
        sums = []
        for j in range(2):
            h = 2 * p + j
            high, low = halves(prefix_state(before, p, j, early_ref, c))
            sums.append(nt(doubled(qk_ref[rows, at(h, 128)]), jnp.concatenate([high, low], axis=1)))
        even, odd = sums
        inverse = 1.0 / (inverse_ref[rows, cols] + jnp.where(left, swap_halves(even), odd))
        ratio = (ratio_ref[rows, cols] + jnp.where(left, even, swap_halves(odd))) * inverse
        ratio_ref[rows, cols] = ratio
        inverse_ref[rows, cols] = inverse
        mixed_ref[rows, cols] = ratio.astype(BF16)


def mean_rows(value):
    return jnp.mean(value, axis=-1, keepdims=True)


def standard(hidden):
    centred = hidden - mean_rows(hidden)
    scale = lax.rsqrt(mean_rows(centred * centred) + EPSILON)
    return centred * scale, scale


def norm_back(grad, normal, scale, gain):
    scaled = grad * gain
    return scale * (scaled - mean_rows(scaled) - normal * mean_rows(scaled * normal))


def column(value):
    return jnp.sum(value, axis=0, keepdims=True)


ORDERS = ((1, 0, 2), (0, 2, 1), (2, 1, 0))
SUBS = 9
COLS = 256


def cell(ref, order, picks):
    at = [slice(None)] * 3
    for axis, pick in zip(order, picks):
        at[axis] = pick
    return ref.at[tuple(at)]


def rest(ref, order, pick):
    return ref.at[pick] if order[1] < order[2] else ref.at[:, pick]


def halved(ref, order, pick, half):
    at = [slice(None)] * 3
    at[order[0]] = pick
    at[1 if order[0] == 0 else 0] = half
    return ref.at[tuple(at)]


def add_blocks(dst, srcs, lead, fresh=False):
    total = 1
    for n in lead:
        total *= n

    def step(k, carry):
        where, rest = [], k
        for n in reversed(lead):
            where.append(lax.rem(rest, n))
            rest = rest // n
        where = tuple(reversed(where))
        value = srcs[0][where] if fresh else dst[where] + srcs[0][where]
        for src in srcs[1:]:
            value = value + src[where]
        dst[where] = value

    lax.fori_loop(0, total, step, None)


SLOTS = (0, 1, 2, 3, 0, 1)


def arrived(ref, sem):
    pltpu.make_async_copy(ref, ref, sem).wait()


class Reduction:
    def __init__(self, stage, sums, first, second, third, done, core_send, core_recv, send, recv, keep,
                 spread_recv, spread_send, final):
        self.stage, self.sums, self.first, self.second, self.third, self.done = stage, sums, first, second, third, done
        self.core_send, self.core_recv, self.send, self.recv, self.keep = core_send, core_recv, send, recv, keep
        self.spread_recv, self.spread_send, self.final = spread_recv, spread_send, final
        self.me = tuple(lax.axis_index(a) for a in AX)
        self.core = lax.axis_index(CORE)
        self.other = 1 - self.core

    def swap(self, g, s, part):
        where = (part,) if g < 2 else (slice(None), slice(None), part)
        return pltpu.make_async_remote_copy(
            src_ref=self.stage.at[(g % 2, s, self.other, *where)], dst_ref=self.sums.at[(SLOTS[g], s, *where)],
            send_sem=self.core_send.at[SLOTS[g], s], recv_sem=self.core_recv.at[SLOTS[g], s],
            device_id={CORE: self.other}, device_id_type=MESH)

    def swaps(self, g):
        for s in range(3):
            for part in range(4):
                self.swap(g, s, part).start()

    def remote(self, src, dst, g, s, stage, k, axis, d):
        pltpu.make_async_remote_copy(
            src_ref=src, dst_ref=dst, send_sem=self.send.at[SLOTS[g], stage] if k < 5 else self.spread_send.at[g],
            recv_sem=self.recv.at[SLOTS[g], s, k] if k < 5 else self.spread_recv.at[g, s],
            device_id={AX[axis]: rot(self.me[axis], d)}, device_id_type=MESH).start()

    def views(self, g, s):
        slot = SLOTS[g]
        return (self.sums.at[slot, s], self.first.at[slot, s], self.second.at[slot, s], self.third.at[slot, s],
                self.done.at[g, s], self.stage.at[g % 2, s, self.core], self.recv.at[slot, s])

    def begin(self, g, s):
        mine, inbox, _, _, _, own, _ = self.views(g, s)
        arrived(mine, self.core_recv.at[SLOTS[g], s])
        arrived(own, self.core_send.at[SLOTS[g], s])
        add_blocks(mine, [own], (4, 4))
        order = ORDERS[s]
        ax = order[0]
        far = rot(self.me[ax], 2)
        lo, hi = pl.ds(0, 2), pl.ds(2, 2)
        self.remote(halved(mine, order, far, lo), inbox.at[0, lo], g, s, 0, 0, ax, 1)
        self.remote(halved(mine, order, far, hi), inbox.at[0, hi], g, s, 0, 1, ax, 3)

    def follow(self, g, s):
        mine, inbox = self.views(g, s)[:2]
        order = ORDERS[s]
        ax = order[0]
        i = self.me[ax]
        lo, hi = pl.ds(0, 2), pl.ds(2, 2)
        self.remote(halved(mine, order, rot(i, 1), hi), inbox.at[1, hi], g, s, 0, 2, ax, 1)
        self.remote(halved(mine, order, rot(i, 3), lo), inbox.at[2, lo], g, s, 0, 2, ax, 3)

    def relay(self, g, s):
        mine, inbox, _, _, _, _, recv = self.views(g, s)
        order = ORDERS[s]
        ax = order[0]
        i = self.me[ax]
        lo, hi = pl.ds(0, 2), pl.ds(2, 2)
        arrived(inbox.at[0, lo], recv.at[0])
        part = halved(mine, order, rot(i, 1), lo)
        add_blocks(part, [inbox.at[0, lo]], (2, 4))
        self.remote(part, inbox.at[1, lo], g, s, 0, 2, ax, 1)
        arrived(inbox.at[0, hi], recv.at[1])
        part = halved(mine, order, rot(i, 3), hi)
        add_blocks(part, [inbox.at[0, hi]], (2, 4))
        self.remote(part, inbox.at[2, hi], g, s, 0, 2, ax, 3)

    def middle(self, g, s):
        mine, inbox, second, _, _, _, recv = self.views(g, s)
        order = ORDERS[s]
        arrived(inbox.at[pl.ds(1, 2)], recv.at[2])
        i, ax = self.me[order[0]], order[1]
        add_blocks(inbox.at[0], [cell(mine, order, (i,)), inbox.at[1], inbox.at[2]], (4,), fresh=True)
        for k, d in enumerate(DIRECT):
            self.remote(rest(inbox.at[0], order, rot(self.me[ax], d)), second.at[k], g, s, 1, 3, ax, d)

    def cleared(self, g):
        arrived(self.first.at[SLOTS[g]], self.send.at[SLOTS[g], 0])

    def last(self, g, s):
        _, inbox, second, third, _, _, recv = self.views(g, s)
        order = ORDERS[s]
        arrived(second, recv.at[3])
        mine = rest(inbox.at[0], order, self.me[order[1]])
        add_blocks(mine, [second.at[k] for k in range(3)], (4,))
        ax = order[2]
        for k, d in enumerate(DIRECT):
            self.remote(mine.at[rot(self.me[ax], d)], third.at[k], g, s, 2, 4, ax, d)

    def spread(self, g, s):
        _, inbox, _, third, done, _, recv = self.views(g, s)
        order = ORDERS[s]
        arrived(third, recv.at[4])
        part = rest(inbox.at[0], order, self.me[order[1]]).at[self.me[order[2]]]
        self.final[g, s] = part[...] + third[0] + third[1] + third[2]
        part = self.final.at[g, s]
        z = self.me[2]
        for k, d in enumerate(DIRECT):
            self.remote(part, done.at[z], g, s, 3, 5, 2, d)
        pltpu.make_async_copy(part, done.at[z], self.keep.at[g]).start()

    def finish(self, g, s):
        third = self.views(g, s)[3]
        arrived(third, self.spread_recv.at[g, s])

    def sent(self, g):
        slot = SLOTS[g]
        arrived(self.second.at[slot], self.send.at[slot, 1])
        arrived(self.third.at[slot], self.send.at[slot, 2])

    def spread_sent(self, g):
        arrived(self.final.at[g], self.keep.at[g])
        arrived(self.third.at[SLOTS[g]], self.spread_send.at[g])

    def each(self, step, g):
        with jax.named_scope(f"{step.__name__} {g}"):
            for s in range(3):
                step(g, s)


def vector_steps(vec, vecs, send, recv):
    me = tuple(lax.axis_index(a) for a in AX)
    core = lax.axis_index(CORE)
    bases = (0, 1, 4, 7)

    def start(stage):
        if stage == 0:
            targets = [{CORE: 1 - core}]
        else:
            ax = stage - 1
            targets = [{AX[ax]: rot(me[ax], d)} for d in DIRECT]
        for k, target in enumerate(targets):
            pltpu.make_async_remote_copy(
                src_ref=vec, dst_ref=vecs.at[bases[stage] + k], send_sem=send.at[stage], recv_sem=recv.at[stage],
                device_id=target, device_id_type=MESH).start()

    def end(stage):
        with jax.named_scope("vector"):
            count = 3 if stage else 1
            part = vecs.at[pl.ds(bases[stage], count)]
            arrived(part, recv.at[stage])
            arrived(part, send.at[stage])
            total = vec[...]
            for k in range(count):
                total = total + vecs[bases[stage] + k]
            vec[...] = total

    return start, end


def suffix_state(after, p, j, late_ref, c):
    body, row = after[p, 2 * j : 2 * j + 2, 0:32].reshape(64, 128), after[p, 0, 32 + j : 33 + j]
    if c == 0:
        h = 2 * p + j
        body, row = body + late_ref[h, 0:64], row + (late_ref[h, 64:65] + late_ref[h, 65:66])
    first = lax.broadcasted_iota(jnp.int32, (64, 128), 0) == 0
    return jnp.concatenate([body, jnp.where(first, jnp.broadcast_to(row, (64, 128)), 0.0)], axis=0)


def attend_back_query(p, act, bufu, early_ref, before, trigs, grads):
    causal, _ = causal_masks()
    left = left_lanes(CHUNK)
    for c in range(2):
        rows = slice(CHUNK * c, CHUNK * c + CHUNK)
        query = []
        for j in range(2):
            h = 2 * p + j
            k = bufu[rows, at(HEADS + h, 128)]
            v, g = act[rows, at(h, 128)], act[rows, at(HEADS + h, 128)]
            high, low = halves(prefix_state(before, p, j, early_ref, c))
            weight = jnp.where(causal, nt(g, v), 0.0).astype(BF16)
            gq = nn(weight, k) + nn(doubled(g), jnp.concatenate([high, low], axis=0))
            gq = gq * trigs[0, rows]
            query.append(gq + swap_halves(gq))
        gate = bufu[ROWS:WIDTH, at(PAIRS * c + p, 128)].astype(F32)
        grads[rows, at(p, 128)] = (jnp.where(left, query[0], query[1]) * gate).astype(BF16)


def attend_back_local(p, act, bufu, trigs, key_ref, value_ref):
    _, flipped = causal_masks()
    left = left_lanes(CHUNK)
    cols = at(p, 128)
    for c in range(2):
        rows = slice(CHUNK * c, CHUNK * c + CHUNK)
        keys, value = [], []
        for j in range(2):
            h = 2 * p + j
            q, k = bufu[rows, at(h, 128)], bufu[rows, at(HEADS + h, 128)]
            v, g = act[rows, at(h, 128)], act[rows, at(HEADS + h, 128)]
            gk = nn(jnp.where(flipped, nt(v, g), 0.0).astype(BF16), q) * trigs[1, rows]
            keys.append(gk + swap_halves(gk))
            value.append(nn(jnp.where(flipped, nt(k, q), 0.0).astype(BF16), g))
        key_ref[rows, cols] = jnp.where(left, keys[0], keys[1])
        value_ref[rows, cols] = jnp.where(left, value[0], swap_halves(value[1]))


def attend_back_later(p, act, bufu, late_ref, after, trigs, ratio_ref, inverse_ref, grads):
    left = left_lanes(CHUNK)
    for c in range(2):
        rows = slice(CHUNK * c, CHUNK * c + CHUNK)
        keys, value = [], []
        for j in range(2):
            h = 2 * p + j
            k, v = bufu[rows, at(HEADS + h, 128)], act[rows, at(h, 128)]
            high, low = halves(suffix_state(after, p, j, late_ref, c))
            gk = nn(doubled(v), jnp.concatenate([high, low], axis=0)) * trigs[1, rows]
            keys.append(gk + swap_halves(gk))
            value.append(nt(doubled(k), jnp.concatenate([high, low], axis=1)))
        cols = at(p, 128)
        gate = bufu[ROWS:WIDTH, at(2 * PAIRS + PAIRS * c + p, 128)].astype(F32)
        gk = (ratio_ref[rows, cols] + jnp.where(left, keys[0], keys[1])) * gate
        grads[rows, at(PAIRS + p, 128)] = gk.astype(BF16)
        gv = inverse_ref[rows, cols] + jnp.where(left, value[0], swap_halves(value[1]))
        grads[rows, at(2 * PAIRS + p, 128)] = gv.astype(BF16)


def layer_kernel(len_ref, bq_in, bk_in, bv_in, bo_in, gain1_in, shift1_in, bdown_in, gain2_in, shift2_in, bup_in,
                 x_hbm, wq_hbm, wk_hbm, wv_hbm, wo_hbm, wup_hbm, wdown_hbm, cot_hbm,
                 block_out, tokens_out, done_out, vec_out, act_spill, slope_spill,
                 x_ref, act, slope, bufu, bufd, trigs, early_ref, late_ref, state, before, pay, after,
                 ratio_ref, inverse_ref, normal_ref, acc_ref, scale_ref, mixed_ref, normed_ref, gffn_ref, vec_ref, rows_ref,
                 bup, turned, stage, sums, first_in, second_in, third_in, final_ref, vecs,
                 load_sem, core_send, core_recv, send, recv, keep_sem, spread_recv, spread_send, vec_send, vec_recv, free_sem, open_sem, *scratch):
    everywhere = ("seq_0", "seq_1", "batch")
    greet(everywhere)
    loads = {}

    def load(name, src, dst):
        copy = pltpu.make_async_copy(src, dst, load_sem.at[len(loads)])
        copy.start()
        loads[name] = copy

    def ready(*names):
        with jax.named_scope("ready"):
            for name in names:
                loads[name].wait()

    def note(k, value):
        vec_ref[k : k + 1, :] += value

    load("x", x_hbm, x_ref)
    for n in range(3):
        cols = pl.ds(256 * n, 256)
        load(f"wv{n}", wv_hbm.at[:, cols], bufd.at[2 * WIDTH : 3 * WIDTH, cols])
        load(f"wk{n}", wk_hbm.at[:, cols], bufd.at[WIDTH : 2 * WIDTH, cols])
    load("wq", wq_hbm, bufd.at[0:WIDTH])
    for k, vector in enumerate((bq_in, bk_in, bv_in, bo_in, gain1_in, shift1_in, bdown_in, gain2_in, shift2_in)):
        rows_ref[k : k + 1, :] = vector[...].reshape(1, WIDTH)
    bup[...] = bup_in[...].reshape(1, HIDDEN)
    bq, bk, bv, bo, gain1, shift1, bdown, gain2, shift2 = (rows_ref.at[k : k + 1] for k in range(9))
    vec_ref[...] = jnp.zeros_like(vec_ref)
    length = len_ref[0]
    start = ROWS * ((lax.axis_index("seq_0") * 4 + lax.axis_index("seq_1")) * 2 + lax.axis_index(CORE))

    def angles(r):
        both, valid = trig_block(start + 128 * r, 128, length)
        trigs[0, at(r, 128)] = both
        trigs[1, at(r, 128)] = both * valid

    loop(ROWS // 128, angles)
    ready("x", "wv0", "wk0")
    load("wup", wup_hbm, bufu)
    wo = bufd.at[3 * WIDTH : HIDDEN]
    load("wo", wo_hbm, wo)
    load("cot", cot_hbm, gffn_ref)
    earlier_sums = Exchange(exchange_steps, state, before, *scratch[: len(EXCHANGE_SCRATCH)])
    later_sums = Exchange(quarter_steps, pay, after, *scratch[len(EXCHANGE_SCRATCH) :])

    def keys(n):
        project_values(n, x_ref, bufd.at[2 * WIDTH : 3 * WIDTH], bv, slope)
        project_soft(n, x_ref, bufd.at[WIDTH : 2 * WIDTH], bk, trigs.at[1], act, HEADS, slope, 9)
        each_of(2, lambda j: state_sums(2 * n + j, act, slope, state, early_ref))
        pl.when(n == 0)(lambda: greeted(everywhere))
        earlier_sums.step(0, n)
        pl.when(n > 0)(lambda: earlier_sums.step(1, n - 1))

    def queries(n):
        project_soft(n, x_ref, bufd.at[0:WIDTH], bq, trigs.at[0], act, 0, slope, 6)
        pl.when(n == 0)(lambda: earlier_sums.step(1, 2))

    def own(p):
        pl.when(lax.rem(p, 2) == 0)(lambda: earlier_sums.step(2, p // 2))
        attend_local(p, act, slope, ratio_ref, inverse_ref)

    def earlier(p):
        pl.when(lax.rem(p, 2) == 0)(lambda: earlier_sums.step(4, p // 2))
        attend_earlier(p, act, early_ref, before, ratio_ref, inverse_ref, mixed_ref)

    loop(3, keys, {n: lambda n=n: ready(f"wv{n + 1}", f"wk{n + 1}") for n in range(2)})
    ready("wq")
    loop(3, queries)
    load("wdown", wdown_hbm.at[0 : 3 * WIDTH], bufd.at[0 : 3 * WIDTH])
    load("qk_out", act, act_spill)
    load("v_out", slope, slope_spill)
    loop(PAIRS, own)
    each_of(3, lambda n: earlier_sums.step(3, n))
    loop(PAIRS, earlier)
    ready("wo")

    def first_norm(r):
        rows = at(r, CHUNK)
        hidden = x_ref[rows].astype(F32) + (nn(mixed_ref[rows], wo[...]) + bo[...])
        normal, scale = standard(hidden)
        normal_ref[rows] = normal
        scale_ref[rows] = jnp.broadcast_to(scale, (CHUNK, 128))
        normed_ref[rows] = (normal * gain1[...] + shift1[...]).astype(BF16)

    loop(ROWS // CHUNK, first_norm)
    load("wdown end", wdown_hbm.at[3 * WIDTH : HIDDEN], wo)
    ready("qk_out", "v_out", "wup", "wdown")

    def feed(t):
        cols = at(t, FEED)
        for r in range(2):
            rows = slice(CHUNK * r, CHUNK * r + CHUNK)
            pre = nn(normed_ref[rows], bufu[:, cols]) + bup[:, cols]
            whole, bell = normal_parts(pre)
            active = (pre * whole).astype(BF16)
            act[rows, cols] = active
            slope[rows, cols] = (whole + pre * bell).astype(BF16)
            acc_ref[rows] = nn(active, bufd[cols]) + jnp.where(t == 0, 0.0, acc_ref[rows])

    loop(3, feed, {1: lambda: ready("wdown end")})
    ready("cot")

    def second_norm(r):
        rows = at(r, CHUNK)
        hidden = normed_ref[rows].astype(F32) + (acc_ref[rows] + bdown[...])
        normal, scale = standard(hidden)
        x_ref[rows] = (normal * gain2[...] + shift2[...]).astype(BF16)
        grad = gffn_ref[rows].astype(F32)
        note(7, column(grad * normal))
        note(8, column(grad))
        back = norm_back(grad, normal, scale, gain2[...])
        acc_ref[rows] = back
        low = back.astype(BF16)
        gffn_ref[rows] = low
        note(6, column(low.astype(F32)))

    loop(ROWS // CHUNK, second_norm)
    load("block", x_ref, block_out)
    red = Reduction(stage, sums, first_in, second_in, third_in, done_out, core_send, core_recv, send, recv, keep_sem,
                    spread_recv, spread_send, final_ref)

    def down_rows(y):
        turned[...] = act[:, at(y, WIDTH)].T
        for n in range(3):
            value = nn(turned[...], gffn_ref[:, 256 * n : 256 * n + 256]).reshape(4, 2, 4, 24, 256)
            for half in range(2):
                unit = 2 * n + half
                for side in range(2):
                    stage[unit // 3, unit % 3, side, y] = value[:, side, :, :, 128 * half : 128 * half + 128]
        for s in range(3):
            red.swap(0, s, y).start()

    loop(4, down_rows)
    red.swaps(1)
    load("v", slope_spill.at[:, 0 : 128 * HEADS], act.at[:, 0 : 128 * HEADS])

    def feed_back(k):
        t = 1 - k
        cols = at(t, TILE)
        total = jnp.zeros((1, TILE), F32)
        for r in range(2):
            rows = slice(CHUNK * r, CHUNK * r + CHUNK)
            gpre = (nt(gffn_ref[rows], bufd[cols]) * slope[rows, cols].astype(F32)).astype(BF16)
            slope[rows, cols] = gpre
            total = total + column(gpre.astype(F32))
            acc_ref[rows] += nt(gpre, bufu[:, cols])
        for half in range(2):
            vec_ref[pl.ds(9 + 2 * t + half, 1), :] = total[:, WIDTH * half : WIDTH * half + WIDTH]

    loads["wo again"] = pltpu.make_async_copy(wo_hbm, wo, load_sem.at[31])

    def down_begun():
        red.each(red.begin, 0)
        loads["wo again"].start()

    loop(2, feed_back, {0: down_begun})
    red.each(red.follow, 0)
    red.each(red.begin, 1)
    ready("block")
    load("x again", x_hbm, x_ref)
    load("wq again", wq_hbm, bufd.at[0:WIDTH])
    load("wk again", wk_hbm, bufd.at[WIDTH : 2 * WIDTH])
    load("wv again", wv_hbm, bufd.at[2 * WIDTH : 3 * WIDTH])
    load("qk", act_spill, bufu.at[0:ROWS])
    gates = []
    for i in range(2):
        for c in range(2):
            gates.append(f"gate {i}{c}")
            load(gates[-1], slope_spill.at[CHUNK * c : CHUNK * c + CHUNK, pl.ds(128 * HEADS + WIDTH * i, WIDTH)],
                 bufu.at[ROWS:WIDTH, pl.ds(2 * WIDTH * i + WIDTH * c, WIDTH)])
    def up_columns(b):
        for n in range(3):
            cols = pl.ds(pl.multiple_of(WIDTH * b + 256 * n, 256), 256)
            value = nn(turned[...], slope[:, cols]).reshape(4, 4, 2, 24, 256)
            for half in range(2):
                unit = 2 * n + half
                for side in range(2):
                    stage[unit // 3, unit % 3, side, :, :, b] = value[:, :, side, :, 128 * half : 128 * half + 128]
        for s in range(3):
            red.swap(2, s, b).start()

    def first_back(r):
        rows = at(r, CHUNK)
        normal = normal_ref[rows]
        scale = scale_ref[rows, 0:1]
        grad = acc_ref[rows]
        note(4, column(grad * normal))
        note(5, column(grad))
        back = norm_back(grad, normal, scale, gain1[...])
        acc_ref[rows] = back
        low = back.astype(BF16)
        gffn_ref[rows] = low
        note(3, column(low.astype(F32)))
        normal_ref[rows] = nt(low, wo[...])

    def heads_back(p):
        cols = at(p, 128)
        lane = lax.broadcasted_iota(jnp.int32, (ROWS, 128), 1)
        left = lane < 64
        gnum = (normal_ref[:, cols] * inverse_ref[:, cols]).astype(BF16).astype(F32)
        product = gnum * ratio_ref[:, cols]
        ends_of = []
        for j in range(2):
            h = 2 * p + j
            mine = jnp.where(left, product, 0.0) if j == 0 else jnp.where(left, 0.0, product)
            gden = jnp.broadcast_to(-jnp.sum(mine, axis=1, keepdims=True), (ROWS, 128))
            high = gden.astype(BF16).astype(F32)
            ends = jnp.where(lane == 64, high, jnp.where(lane == 65, gden - high, 0.0))
            grad = jnp.where(left, gnum if j == 0 else swap_halves(gnum), ends).astype(BF16)
            act[:, at(HEADS + h, 128)] = grad
            late = tn(grad[CHUNK:ROWS], bufu[CHUNK:ROWS, at(h, 128)])
            late_ref[h] = late[0:72]
            both = late + tn(grad[0:CHUNK], bufu[0:CHUNK, at(h, 128)])
            for half in range(2):
                pay[p, 2 * j + half, 0:32] = both[32 * half : 32 * half + 32]
                pay[p, 2 * j + half, 32:40] = jnp.zeros((8, 128), F32)
            ends_of.append(both[64:65] + both[65:66])
        for j in range(2):
            pay[p, 0, 32 + j : 33 + j] = ends_of[j]

    def query_back(p):
        attend_back_query(p, act, bufu, early_ref, before, trigs, slope)

    def own_back(p):
        attend_back_local(p, act, bufu, trigs, ratio_ref, inverse_ref)

    def later(p):
        attend_back_later(p, act, bufu, late_ref, after, trigs, ratio_ref, inverse_ref, slope)

    def back(r):
        rows = at(r, CHUNK)
        total = acc_ref[rows]
        for i in range(3):
            total = total + nt(slope[rows, WIDTH * i : WIDTH * i + WIDTH], bufd[WIDTH * i : WIDTH * i + WIDTH])
        acc_ref[rows] = total

    def product(rhs, base, g, b0, n):
        with jax.named_scope("product"):
            value = nn(turned[...], rhs[:, at(base + n, 256)]).reshape(4, 4, 2, 24, 256)
            for part in range(2):
                unit = 2 * n + part
                half, s = unit // 3, lax.rem(unit, 3)
                for side in range(2):
                    stage[g % 2, s, side, :, :, b0 + half] = value[:, :, side, :, 128 * part : 128 * part + 128]
                red.swap(g, s, b0 + half).start()

    def free(k):
        red.cleared(k)
        pl.semaphore_signal(free_sem.at[k], inc=1, device_id={CORE: red.other}, device_id_type=MESH)

    def freed(k):
        with jax.named_scope("freed"):
            pl.semaphore_wait(free_sem.at[k], 1)

    def release(k):
        red.sent(k)
        for axis in everywhere:
            for d in DIRECT:
                pl.semaphore_signal(open_sem.at[k], inc=1, device_id={axis: rot(lax.axis_index(axis), d)},
                                    device_id_type=MESH)

    def released(k):
        with jax.named_scope("released"):
            pl.semaphore_wait(open_sem.at[k], 9)

    ready("wo again")
    loop(ROWS // CHUNK, first_back)
    red.each(red.relay, 0)
    red.each(red.follow, 1)
    each_of(3, lambda n: earlier_sums.step(5, n))
    ready("qk", "v")

    def heads_sent(p):
        heads_back(p)

        @pl.when(lax.rem(p, 2) == 1)
        def _():
            later_sums.step(0, p // 2)
            pl.when(p > 1)(lambda: later_sums.step(1, p // 2 - 1))

    loop(PAIRS, heads_sent)
    turned[...] = normed_ref[...].T

    def up_first():
        later_sums.step(1, 2)
        red.each(red.relay, 1)

    loop(4, up_columns, {0: up_first, 2: lambda: red.each(red.middle, 0)})
    red.swaps(3)
    later_sums.step(2, 0)
    free(0)
    ready(*gates)

    def query_two(n):
        query_back(2 * n)
        query_back(2 * n + 1)

    def query_second():
        later_sums.step(2, 1)
        red.each(red.begin, 2)

    def query_fourth():
        later_sums.step(2, 2)
        later_sums.step(6, 0)
        red.each(red.middle, 1)

    loop(3, query_two, {0: query_second, 1: query_fourth})
    red.each(red.begin, 3)
    red.each(red.follow, 2)
    later_sums.step(6, 1)
    red.each(red.last, 0)
    free(1)
    turned[...] = mixed_ref[...].T
    freed(0)
    loop(3, lambda n: product(gffn_ref, 0, 4, 0, n))
    later_sums.step(6, 2)
    ready("x again")
    turned[...] = x_ref[...].T
    loop(3, lambda n: product(slope, 0, 4, 2, n))

    def own_two(n):
        own_back(2 * n)
        own_back(2 * n + 1)

    def own_fourth():
        red.each(red.relay, 2)
        red.each(red.follow, 3)
        red.each(red.last, 1)

    loop(3, own_two, {1: own_fourth})
    red.each(red.relay, 3)
    each_of(3, lambda n: later_sums.step(3, n))
    red.each(red.spread, 0)
    release(0)
    freed(1)

    def keys_values(n):
        later_sums.step(4, n)
        each_of(2, lambda j: later(2 * n + j))
        each_of(2, lambda i: product(slope, 3 + 3 * i, 5, 2 * i, n))

    def keys_first():
        red.each(red.middle, 2)
        red.each(red.spread, 1)
        release(1)

    def keys_second():
        released(0)
        red.each(red.begin, 4)
        red.each(red.middle, 3)

    loop(3, keys_values, {0: keys_first, 1: keys_second})
    red.each(red.follow, 4)
    for i in range(3):
        note(i, column(slope[:, WIDTH * i : WIDTH * i + WIDTH].astype(F32)))
    vector_start, vector_end = vector_steps(vec_ref, vecs, vec_send, vec_recv)
    vector_start(0)
    released(1)
    red.each(red.begin, 5)
    red.each(red.relay, 4)
    vector_end(0)
    ready("wq again", "wk again", "wv again")

    def back_first():
        red.each(red.follow, 5)
        red.each(red.last, 2)

    loop(ROWS // CHUNK, back, {0: back_first})
    load("tokens", acc_ref, tokens_out)
    red.each(red.relay, 5)
    vector_start(1)
    red.each(red.middle, 4)
    red.each(red.last, 3)
    red.each(red.spread, 2)
    vector_end(1)
    vector_start(2)
    red.each(red.middle, 5)
    red.each(red.last, 4)
    red.each(red.spread, 3)
    vector_end(2)
    vector_start(3)
    red.each(red.last, 5)
    red.each(red.spread, 4)
    vector_end(3)
    load("vec", vec_ref, vec_out)
    red.each(red.spread, 5)
    for g in range(6):
        red.each(red.finish, g)
        red.spread_sent(g)
    for g in range(2, 6):
        red.cleared(g)
        red.sent(g)
    each_of(3, lambda n: later_sums.step(5, n))
    ready("tokens", "vec")


def final_kernel(done, vecs, tokens, block, block_out, tokens_out, out_q, out_bq, out_k, out_bk, out_v, out_bv, out_o,
                 out_bo, out_g1, out_s1, out_up, out_bup, out_down, out_bdown, out_g2, out_s2):
    tokens_out[...] = tokens[...]
    block_out[...] = block[...]
    for s in range(3):
        for b in range(4):
            for half in range(2):
                at_col = 384 * half + 128 * s
                out_down[24 * b : 24 * b + 24, at_col : at_col + 128] = done[half, s, b]
                out_up[:, 768 * b + at_col : 768 * b + at_col + 128] = done[2 + half, s, b]
            cols = slice(384 * (b % 2) + 128 * s, 384 * (b % 2) + 128 * s + 128)
            (out_o, out_q)[b // 2][:, cols] = done[4, s, b]
            (out_k, out_v)[b // 2][:, cols] = done[5, s, b]
    seq = (lax.axis_index("seq_0") * 4 + lax.axis_index("seq_1")) * 2 + lax.axis_index(CORE)
    values = vecs[...]
    mine = pltpu.roll(values, lax.rem(WIDTH - 24 * seq, WIDTH), 1)
    for k, out in enumerate((out_bq, out_bk, out_bv, out_bo, out_g1, out_s1, out_bdown, out_g2, out_s2)):
        out[...] = mine[k, 0:24]
    spun = pltpu.roll(values, lax.rem(WIDTH - 96 * lax.rem(seq, 8), WIDTH), 1)
    row = lax.broadcasted_iota(jnp.int32, (16, WIDTH), 0)
    out_bup[...] = jnp.sum(jnp.where(row == 9 + seq // 8, spun, 0.0), axis=0)[0:96]


def on_device(tokens, lengths, w_query, b_query, w_key, b_key, w_value, b_value, w_out, b_out, gain_one, shift_one,
              w_up, b_up, w_down, b_down, gain_two, shift_two, cotangent):
    vmem = pl.BlockSpec(memory_space=VMEM)
    smem = pl.BlockSpec(memory_space=pltpu.SMEM)
    anywhere = pl.BlockSpec(memory_space=pl.ANY)
    out = jax.ShapeDtypeStruct
    wide16, wide32, long16 = ((ROWS, WIDTH), BF16), ((ROWS, WIDTH), F32), ((ROWS, HIDDEN), BF16)
    per_head, packed = ((HEADS, 72, 128), F32), ((PAIRS, 136, 128), F32)
    quarters = ((PAIRS, 4, 40, 128), F32)
    vector = ((16, WIDTH), F32)
    finished = ((6, 3, 4, 24, 128), F32)
    block, tokens_grad, done, sums, _, _ = pl.pallas_call(
        layer_kernel,
        out_shape=[out(*shape) for shape in (wide16, wide32, finished, vector, long16, long16)],
        in_specs=[smem] + [vmem] * 10 + [anywhere] * 8,
        out_specs=[anywhere] * 6,
        scratch_shapes=[VMEM(*shape) for shape in (
            wide16, long16, long16, ((WIDTH, HIDDEN), BF16), ((HIDDEN, WIDTH), BF16),
            ((2, ROWS, 128), F32), per_head, per_head, packed, packed, quarters, quarters,
            wide32, wide32, wide32, wide32, ((ROWS, 128), F32), wide16, wide16, wide16, vector, vector,
            ((1, HIDDEN), F32), ((WIDTH, ROWS), BF16),
            ((2, 3, 2, 4, 4, 4, 24, 128), F32), ((4, 3, 4, 4, 4, 24, 128), F32), ((4, 3, 3, 4, 4, 24, 128), F32),
            ((4, 3, 3, 4, 24, 128), F32), ((4, 3, 3, 24, 128), F32), ((6, 3, 24, 128), F32), ((10, 16, WIDTH), F32))]
        + [pltpu.SemaphoreType.DMA((32,)), pltpu.SemaphoreType.DMA((4, 3)), pltpu.SemaphoreType.DMA((4, 3)),
           pltpu.SemaphoreType.DMA((4, 3)), pltpu.SemaphoreType.DMA((4, 3, 5)), pltpu.SemaphoreType.DMA((6,)), pltpu.SemaphoreType.DMA((6, 3)),
           pltpu.SemaphoreType.DMA((6,)),
           pltpu.SemaphoreType.DMA((4,)), pltpu.SemaphoreType.DMA((4,)), pltpu.SemaphoreType.REGULAR((2,)), pltpu.SemaphoreType.REGULAR((2,))]
        + EXCHANGE_SCRATCH + QUARTER_SCRATCH,
        compiler_params=pltpu.CompilerParams(collective_id=1, has_side_effects=True, vmem_limit_bytes=LIMIT),
    )(lengths, b_query, b_key, b_value, b_out, gain_one, shift_one, b_down, gain_two, shift_two, b_up,
      tokens[0], w_query, w_key, w_value, w_out, w_up, w_down, cotangent[0])
    square_share, vector_share = out((24, WIDTH), F32), out((24,), F32)
    results = pl.pallas_call(
        final_kernel,
        out_shape=[out(*wide16), out(*wide32)] + [square_share, vector_share] * 4 + [vector_share] * 2
        + [out((24, HIDDEN), F32), out((96,), F32), out((96, WIDTH), F32)] + [vector_share] * 3,
        in_specs=[vmem] * 4,
        out_specs=[vmem] * 18,
        compiler_params=pltpu.CompilerParams(vmem_limit_bytes=LIMIT),
    )(done, sums, tokens_grad, block)
    return (results[0][None], results[1][None], *results[2:])


def solution(mesh):
    torus = Mesh(mesh.devices.reshape(4, 4, 2, mesh.shape["batch"]), (*SEQ, "batch"))
    rows, shares = P("batch", SEQ, None), P(SEQ, None)
    return jax.shard_map(
        on_device,
        mesh=torus,
        in_specs=(rows, P("batch")) + (P(),) * 16 + (rows,),
        out_specs=(rows, rows) + (shares, P(SEQ)) * 4 + (P(SEQ), P(SEQ)) + (shares, P(SEQ)) * 2 + (P(SEQ), P(SEQ)),
        check_vma=False,
    )
```

profile of v0, /device:TPU:0, one launch (start us, length us, event | category | flops | bytes accessed | tf_op | source)
XLA Modules:
  0.0 124.1 jit_solution(8008471694997494544)
XLA Ops:
  1.3 118.9 %shard_map.322 = (bf16[512,768]{1,0:T(8,128)(2,1)}, f32[512,768]{1,0:T(8,128)}, f32[6,3,4,24,128]{4,3,2,1,0:T(8,128)}, f32[16,768]{1,0:T(8,128)}, bf16[512,3072]{1,0:T(8,128)(2,1)}, /*index=5*/bf16[512,3072]{1,0:T(8,128)(2,1)}) custom-call(s32[1]{0:T(128)S(6)} %copy.37.len_ref, f32[768]{0:T(1024)} %bq_in.1, f32[768]{0:T(1024)} %bk_in.1, f32[768]{0:T(1024)} %bv_in.1, ...), custom_call_target="tpu_custom_call" | custom-call | tf_op jit(solution)/shard_map/pallas_call | solution.py:1101
  120.2 3.8 %shard_map.323 = (bf16[512,768]{1,0:T(8,128)(2,1)}, f32[512,768]{1,0:T(8,128)}, f32[24,768]{1,0:T(8,128)}, f32[24]{0:T(128)}, f32[24,768]{1,0:T(8,128)}, /*index...) custom-call(f32[6,3,4,24,128]{4,3,2,1,0:T(8,128)} %get-tuple-element, ...), custom_call_target="tpu_custom_call" | custom-call | tf_op jit(solution)/shard_map/pallas_call | solution.py:1122
where the time goes:
time: 124 us
  Pallas kernels  123 us (99%)
  between operations  1.47 us (1%)
    pallas_call x1, Pallas kernels, on_device(): pl.pallas_call(layer_kernel, out_shape=[out(*shape) for shape in (wide16,...  119 us
    pallas_call x1, Pallas kernels, on_device(): pl.pallas_call(final_kernel, out_shape=[out(*wide16), out(*wide32)] + [sq...  3.77 us

commit v1 on v0

--- a/solution.py
+++ b/solution.py
@@ -22,7 +22,7 @@
 HEADS = 12
 PAIRS = 6
 CHUNK = 256
-FEED = 1024
+FEED = 1536
 TILE = 1536
 VMEM = pltpu.VMEM
 LIMIT = 63 * 2**20
@@ -96,8 +96,8 @@
 
 def trig_block(first, rows, length):
     position = first + lax.broadcasted_iota(jnp.int32, (rows, 128), 0)
-    size = lax.broadcast_in_dim(length, (rows, 128), ()).astype(F32)
-    angle = HALF_PI * jnp.minimum(position + 1, length).astype(F32) / size
+    length = jnp.broadcast_to(length, (rows, 128))
+    angle = HALF_PI * jnp.minimum(position + 1, length).astype(F32) / length.astype(F32)
     both = sine(jnp.where(left_lanes(rows), (HALF_PI - angle) + HALF_PI_REST, angle))
     return both, (position < length).astype(F32)
 
@@ -417,23 +417,14 @@
     return ref.at[tuple(at)]
 
 
-def add_blocks(dst, srcs, lead, fresh=False):
-    total = 1
-    for n in lead:
-        total *= n
-
+def add_blocks(dst, srcs, count, fresh=False):
     def step(k, carry):
-        where, rest = [], k
-        for n in reversed(lead):
-            where.append(lax.rem(rest, n))
-            rest = rest // n
-        where = tuple(reversed(where))
-        value = srcs[0][where] if fresh else dst[where] + srcs[0][where]
+        value = srcs[0][k] if fresh else dst[k] + srcs[0][k]
         for src in srcs[1:]:
-            value = value + src[where]
-        dst[where] = value
-
-    lax.fori_loop(0, total, step, None)
+            value = value + src[k]
+        dst[k] = value
+
+    lax.fori_loop(0, count, step, None)
 
 
 SLOTS = (0, 1, 2, 3, 0, 1)
@@ -480,7 +471,7 @@
         mine, inbox, _, _, _, own, _ = self.views(g, s)
         arrived(mine, self.core_recv.at[SLOTS[g], s])
         arrived(own, self.core_send.at[SLOTS[g], s])
-        add_blocks(mine, [own], (4, 4))
+        add_blocks(mine, [own], 4)
         order = ORDERS[s]
         ax = order[0]
         far = rot(self.me[ax], 2)
@@ -505,11 +496,11 @@
         lo, hi = pl.ds(0, 2), pl.ds(2, 2)
         arrived(inbox.at[0, lo], recv.at[0])
         part = halved(mine, order, rot(i, 1), lo)
-        add_blocks(part, [inbox.at[0, lo]], (2, 4))
+        add_blocks(part, [inbox.at[0, lo]], 2)
         self.remote(part, inbox.at[1, lo], g, s, 0, 2, ax, 1)
         arrived(inbox.at[0, hi], recv.at[1])
         part = halved(mine, order, rot(i, 3), hi)
-        add_blocks(part, [inbox.at[0, hi]], (2, 4))
+        add_blocks(part, [inbox.at[0, hi]], 2)
         self.remote(part, inbox.at[2, hi], g, s, 0, 2, ax, 3)
 
     def middle(self, g, s):
@@ -517,7 +508,7 @@
         order = ORDERS[s]
         arrived(inbox.at[pl.ds(1, 2)], recv.at[2])
         i, ax = self.me[order[0]], order[1]
-        add_blocks(inbox.at[0], [cell(mine, order, (i,)), inbox.at[1], inbox.at[2]], (4,), fresh=True)
+        add_blocks(inbox.at[0], [cell(mine, order, (i,)), inbox.at[1], inbox.at[2]], 4, fresh=True)
         for k, d in enumerate(DIRECT):
             self.remote(rest(inbox.at[0], order, rot(self.me[ax], d)), second.at[k], g, s, 1, 3, ax, d)
 
@@ -529,7 +520,7 @@
         order = ORDERS[s]
         arrived(second, recv.at[3])
         mine = rest(inbox.at[0], order, self.me[order[1]])
-        add_blocks(mine, [second.at[k] for k in range(3)], (4,))
+        mine[...] = mine[...] + second[0] + second[1] + second[2]
         ax = order[2]
         for k, d in enumerate(DIRECT):
             self.remote(mine.at[rot(self.me[ax], d)], third.at[k], g, s, 2, 4, ax, d)
@@ -568,29 +559,35 @@
 def vector_steps(vec, vecs, send, recv):
     me = tuple(lax.axis_index(a) for a in AX)
     core = lax.axis_index(CORE)
-    bases = (0, 1, 4, 7)
+    other = 1 - core
+    bases = (0, 1, 4, 7, 10)
+    mine = vec.at[pl.ds(pl.multiple_of(8 * core, 8), 8)]
+    theirs = vec.at[pl.ds(pl.multiple_of(8 * other, 8), 8)]
 
     def start(stage):
-        if stage == 0:
-            targets = [{CORE: 1 - core}]
+        source = theirs if stage == 0 else mine
+        if stage in (0, 4):
+            targets = [{CORE: other}]
         else:
             ax = stage - 1
             targets = [{AX[ax]: rot(me[ax], d)} for d in DIRECT]
         for k, target in enumerate(targets):
             pltpu.make_async_remote_copy(
-                src_ref=vec, dst_ref=vecs.at[bases[stage] + k], send_sem=send.at[stage], recv_sem=recv.at[stage],
-                device_id=target, device_id_type=MESH).start()
+                src_ref=source, dst_ref=vecs.at[bases[stage] + k],
+                send_sem=send.at[stage], recv_sem=recv.at[stage], device_id=target, device_id_type=MESH).start()
 
     def end(stage):
         with jax.named_scope("vector"):
-            count = 3 if stage else 1
-            part = vecs.at[pl.ds(bases[stage], count)]
+            part = vecs.at[pl.ds(bases[stage], 3)] if stage in (1, 2, 3) else vecs.at[pl.ds(0, 1)]
             arrived(part, recv.at[stage])
             arrived(part, send.at[stage])
-            total = vec[...]
-            for k in range(count):
-                total = total + vecs[bases[stage] + k]
-            vec[...] = total
+            if stage < 4:
+                total = mine[...]
+                for k in range(3 if stage else 1):
+                    total = total + vecs[bases[stage] + k]
+                mine[...] = total
+            else:
+                theirs[...] = vecs[10]
 
     return start, end
 
@@ -692,11 +689,11 @@
         load(f"wk{n}", wk_hbm.at[:, cols], bufd.at[WIDTH : 2 * WIDTH, cols])
     load("wq", wq_hbm, bufd.at[0:WIDTH])
     for k, vector in enumerate((bq_in, bk_in, bv_in, bo_in, gain1_in, shift1_in, bdown_in, gain2_in, shift2_in)):
-        rows_ref[k : k + 1, :] = vector[...].reshape(1, WIDTH)
-    bup[...] = bup_in[...].reshape(1, HIDDEN)
+        load(f"row {k}", vector, rows_ref.at[k])
+    load("bup", bup_in, bup.at[0])
     bq, bk, bv, bo, gain1, shift1, bdown, gain2, shift2 = (rows_ref.at[k : k + 1] for k in range(9))
     vec_ref[...] = jnp.zeros_like(vec_ref)
-    length = len_ref[0]
+    length = len_ref[...].reshape(1, 1)
     start = ROWS * ((lax.axis_index("seq_0") * 4 + lax.axis_index("seq_1")) * 2 + lax.axis_index(CORE))
 
     def angles(r):
@@ -705,7 +702,7 @@
         trigs[1, at(r, 128)] = both * valid
 
     loop(ROWS // 128, angles)
-    ready("x", "wv0", "wk0")
+    ready("x", "wv0", "wk0", *(f"row {k}" for k in range(9)), "bup")
     load("wup", wup_hbm, bufu)
     wo = bufd.at[3 * WIDTH : HIDDEN]
     load("wo", wo_hbm, wo)
@@ -716,10 +713,10 @@
     def keys(n):
         project_values(n, x_ref, bufd.at[2 * WIDTH : 3 * WIDTH], bv, slope)
         project_soft(n, x_ref, bufd.at[WIDTH : 2 * WIDTH], bk, trigs.at[1], act, HEADS, slope, 9)
+        pl.when(n == 0)(lambda: greeted(everywhere))
+        pl.when(n > 0)(lambda: earlier_sums.step(1, n - 1))
         each_of(2, lambda j: state_sums(2 * n + j, act, slope, state, early_ref))
-        pl.when(n == 0)(lambda: greeted(everywhere))
         earlier_sums.step(0, n)
-        pl.when(n > 0)(lambda: earlier_sums.step(1, n - 1))
 
     def queries(n):
         project_soft(n, x_ref, bufd.at[0:WIDTH], bq, trigs.at[0], act, 0, slope, 6)
@@ -767,7 +764,7 @@
             slope[rows, cols] = (whole + pre * bell).astype(BF16)
             acc_ref[rows] = nn(active, bufd[cols]) + jnp.where(t == 0, 0.0, acc_ref[rows])
 
-    loop(3, feed, {1: lambda: ready("wdown end")})
+    loop(2, feed, {0: lambda: ready("wdown end")})
     ready("cot")
 
     def second_norm(r):
@@ -817,7 +814,7 @@
         for half in range(2):
             vec_ref[pl.ds(9 + 2 * t + half, 1), :] = total[:, WIDTH * half : WIDTH * half + WIDTH]
 
-    loads["wo again"] = pltpu.make_async_copy(wo_hbm, wo, load_sem.at[31])
+    loads["wo again"] = pltpu.make_async_copy(wo_hbm, wo, load_sem.at[39])
 
     def down_begun():
         red.each(red.begin, 0)
@@ -1010,37 +1007,37 @@
         each_of(2, lambda i: product(slope, 3 + 3 * i, 5, 2 * i, n))
 
     def keys_first():
+        released(0)
+        red.each(red.begin, 4)
         red.each(red.middle, 2)
+
+    def keys_second():
         red.each(red.spread, 1)
         release(1)
-
-    def keys_second():
-        released(0)
-        red.each(red.begin, 4)
         red.each(red.middle, 3)
 
     loop(3, keys_values, {0: keys_first, 1: keys_second})
-    red.each(red.follow, 4)
     for i in range(3):
         note(i, column(slope[:, WIDTH * i : WIDTH * i + WIDTH].astype(F32)))
     vector_start, vector_end = vector_steps(vec_ref, vecs, vec_send, vec_recv)
     vector_start(0)
     released(1)
     red.each(red.begin, 5)
-    red.each(red.relay, 4)
     vector_end(0)
+    vector_start(1)
     ready("wq again", "wk again", "wv again")
 
     def back_first():
-        red.each(red.follow, 5)
+        red.each(red.follow, 4)
+        red.each(red.relay, 4)
         red.each(red.last, 2)
 
     loop(ROWS // CHUNK, back, {0: back_first})
     load("tokens", acc_ref, tokens_out)
     red.each(red.relay, 5)
-    vector_start(1)
+    red.each(red.follow, 5)
+    red.each(red.last, 3)
     red.each(red.middle, 4)
-    red.each(red.last, 3)
     red.each(red.spread, 2)
     vector_end(1)
     vector_start(2)
@@ -1051,9 +1048,11 @@
     vector_start(3)
     red.each(red.last, 5)
     red.each(red.spread, 4)
+    red.each(red.spread, 5)
     vector_end(3)
+    vector_start(4)
+    vector_end(4)
     load("vec", vec_ref, vec_out)
-    red.each(red.spread, 5)
     for g in range(6):
         red.each(red.finish, g)
         red.spread_sent(g)
@@ -1090,7 +1089,6 @@
 def on_device(tokens, lengths, w_query, b_query, w_key, b_key, w_value, b_value, w_out, b_out, gain_one, shift_one,
               w_up, b_up, w_down, b_down, gain_two, shift_two, cotangent):
     vmem = pl.BlockSpec(memory_space=VMEM)
-    smem = pl.BlockSpec(memory_space=pltpu.SMEM)
     anywhere = pl.BlockSpec(memory_space=pl.ANY)
     out = jax.ShapeDtypeStruct
     wide16, wide32, long16 = ((ROWS, WIDTH), BF16), ((ROWS, WIDTH), F32), ((ROWS, HIDDEN), BF16)
@@ -1101,7 +1099,7 @@
     block, tokens_grad, done, sums, _, _ = pl.pallas_call(
         layer_kernel,
         out_shape=[out(*shape) for shape in (wide16, wide32, finished, vector, long16, long16)],
-        in_specs=[smem] + [vmem] * 10 + [anywhere] * 8,
+        in_specs=[vmem] + [anywhere] * 18,
         out_specs=[anywhere] * 6,
         scratch_shapes=[VMEM(*shape) for shape in (
             wide16, long16, long16, ((WIDTH, HIDDEN), BF16), ((HIDDEN, WIDTH), BF16),
@@ -1109,11 +1107,11 @@
             wide32, wide32, wide32, wide32, ((ROWS, 128), F32), wide16, wide16, wide16, vector, vector,
             ((1, HIDDEN), F32), ((WIDTH, ROWS), BF16),
             ((2, 3, 2, 4, 4, 4, 24, 128), F32), ((4, 3, 4, 4, 4, 24, 128), F32), ((4, 3, 3, 4, 4, 24, 128), F32),
-            ((4, 3, 3, 4, 24, 128), F32), ((4, 3, 3, 24, 128), F32), ((6, 3, 24, 128), F32), ((10, 16, WIDTH), F32))]
-        + [pltpu.SemaphoreType.DMA((32,)), pltpu.SemaphoreType.DMA((4, 3)), pltpu.SemaphoreType.DMA((4, 3)),
+            ((4, 3, 3, 4, 24, 128), F32), ((4, 3, 3, 24, 128), F32), ((6, 3, 24, 128), F32), ((11, 8, WIDTH), F32))]
+        + [pltpu.SemaphoreType.DMA((40,)), pltpu.SemaphoreType.DMA((4, 3)), pltpu.SemaphoreType.DMA((4, 3)),
            pltpu.SemaphoreType.DMA((4, 3)), pltpu.SemaphoreType.DMA((4, 3, 5)), pltpu.SemaphoreType.DMA((6,)), pltpu.SemaphoreType.DMA((6, 3)),
            pltpu.SemaphoreType.DMA((6,)),
-           pltpu.SemaphoreType.DMA((4,)), pltpu.SemaphoreType.DMA((4,)), pltpu.SemaphoreType.REGULAR((2,)), pltpu.SemaphoreType.REGULAR((2,))]
+           pltpu.SemaphoreType.DMA((5,)), pltpu.SemaphoreType.DMA((5,)), pltpu.SemaphoreType.REGULAR((2,)), pltpu.SemaphoreType.REGULAR((2,))]
         + EXCHANGE_SCRATCH + QUARTER_SCRATCH,
         compiler_params=pltpu.CompilerParams(collective_id=1, has_side_effects=True, vmem_limit_bytes=LIMIT),
     )(lengths, b_query, b_key, b_value, b_out, gain_one, shift_one, b_down, gain_two, shift_two, b_up,

time: 124 us -> 120 us (0.968)
  Pallas kernels: 123 us -> 119 us
    pallas_call x1, Pallas kernels: 119 us -> 115 us  [on_device(): pl.pallas_call(layer_kernel, out_shape=[out(*shape) for shape in (wide16,...]
where the time goes in v1:
time: 120 us
  Pallas kernels  119 us (99%)
  between operations  1.47 us (1%)
    pallas_call x1, Pallas kernels, on_device(): pl.pallas_call(layer_kernel, out_shape=[out(*shape) for shape in (wide16,...  115 us
    pallas_call x1, Pallas kernels, on_device(): pl.pallas_call(final_kernel, out_shape=[out(*wide16), out(*wide32)] + [sq...  3.77 us

profile of v1, /device:TPU:0, one launch (start us, length us, event | category | flops | bytes accessed | tf_op | source)
XLA Modules:
  0.0 120.2 jit_solution(18372161927107287889)
XLA Ops:
  1.3 115.0 %shard_map.322 = (bf16[512,768]{1,0:T(8,128)(2,1)}, f32[512,768]{1,0:T(8,128)}, f32[6,3,4,24,128]{4,3,2,1,0:T(8,128)}, f32[16,768]{1,0:T(8,128)}, bf16[512,3072]{1,0:T(8,128)(2,1)}, /*index=5*/bf16[512,3072]{1,0:T(8,128)(2,1)}) custom-call(s32[1]{0:T(128)S(6)} %copy.37.len_ref, f32[768]{0:T(1024)} %bq_in.1, f32[768]{0:T(1024)} %bk_in.1, f32[768]{0:T(1024)} %bv_in.1, ...), custom_call_target="tpu_custom_call" | custom-call | tf_op jit(solution)/shard_map/pallas_call | solution.py:1099
  116.3 3.8 %shard_map.323 = (bf16[512,768]{1,0:T(8,128)(2,1)}, f32[512,768]{1,0:T(8,128)}, f32[24,768]{1,0:T(8,128)}, f32[24]{0:T(128)}, f32[24,768]{1,0:T(8,128)}, /*index...) custom-call(f32[6,3,4,24,128]{4,3,2,1,0:T(8,128)} %get-tuple-element, ...), custom_call_target="tpu_custom_call" | custom-call | tf_op jit(solution)/shard_map/pallas_call | solution.py:1120

commit v2 on v1

--- a/solution.py
+++ b/solution.py
@@ -394,7 +394,8 @@
     return jnp.sum(value, axis=0, keepdims=True)
 
 
-ORDERS = ((1, 0, 2), (0, 2, 1), (2, 1, 0))
+USUAL = ((1, 0, 2), (0, 2, 1), (2, 1, 0))
+ORDERS = (USUAL, USUAL, (USUAL[0], USUAL[1], (2, 0, 1)), (USUAL[0], (0, 1, 2), USUAL[2]), USUAL, USUAL)
 SUBS = 9
 COLS = 256
 
@@ -436,10 +437,10 @@
 
 class Reduction:
     def __init__(self, stage, sums, first, second, third, done, core_send, core_recv, send, recv, keep,
-                 spread_recv, spread_send, final):
+                 spread_recv, spread_send, third_recv, final):
         self.stage, self.sums, self.first, self.second, self.third, self.done = stage, sums, first, second, third, done
         self.core_send, self.core_recv, self.send, self.recv, self.keep = core_send, core_recv, send, recv, keep
-        self.spread_recv, self.spread_send, self.final = spread_recv, spread_send, final
+        self.spread_recv, self.spread_send, self.third_recv, self.final = spread_recv, spread_send, third_recv, final
         self.me = tuple(lax.axis_index(a) for a in AX)
         self.core = lax.axis_index(CORE)
         self.other = 1 - self.core
@@ -459,7 +460,8 @@
     def remote(self, src, dst, g, s, stage, k, axis, d):
         pltpu.make_async_remote_copy(
             src_ref=src, dst_ref=dst, send_sem=self.send.at[SLOTS[g], stage] if k < 5 else self.spread_send.at[g],
-            recv_sem=self.recv.at[SLOTS[g], s, k] if k < 5 else self.spread_recv.at[g, s],
+            recv_sem=(self.recv.at[SLOTS[g], s, k] if k < 4 else
+                      self.third_recv.at[SLOTS[g]] if k == 4 else self.spread_recv.at[g]),
             device_id={AX[axis]: rot(self.me[axis], d)}, device_id_type=MESH).start()
 
     def views(self, g, s):
@@ -472,7 +474,7 @@
         arrived(mine, self.core_recv.at[SLOTS[g], s])
         arrived(own, self.core_send.at[SLOTS[g], s])
         add_blocks(mine, [own], 4)
-        order = ORDERS[s]
+        order = ORDERS[g][s]
         ax = order[0]
         far = rot(self.me[ax], 2)
         lo, hi = pl.ds(0, 2), pl.ds(2, 2)
@@ -481,7 +483,7 @@
 
     def follow(self, g, s):
         mine, inbox = self.views(g, s)[:2]
-        order = ORDERS[s]
+        order = ORDERS[g][s]
         ax = order[0]
         i = self.me[ax]
         lo, hi = pl.ds(0, 2), pl.ds(2, 2)
@@ -490,7 +492,7 @@
 
     def relay(self, g, s):
         mine, inbox, _, _, _, _, recv = self.views(g, s)
-        order = ORDERS[s]
+        order = ORDERS[g][s]
         ax = order[0]
         i = self.me[ax]
         lo, hi = pl.ds(0, 2), pl.ds(2, 2)
@@ -505,7 +507,7 @@
 
     def middle(self, g, s):
         mine, inbox, second, _, _, _, recv = self.views(g, s)
-        order = ORDERS[s]
+        order = ORDERS[g][s]
         arrived(inbox.at[pl.ds(1, 2)], recv.at[2])
         i, ax = self.me[order[0]], order[1]
         add_blocks(inbox.at[0], [cell(mine, order, (i,)), inbox.at[1], inbox.at[2]], 4, fresh=True)
@@ -517,7 +519,7 @@
 
     def last(self, g, s):
         _, inbox, second, third, _, _, recv = self.views(g, s)
-        order = ORDERS[s]
+        order = ORDERS[g][s]
         arrived(second, recv.at[3])
         mine = rest(inbox.at[0], order, self.me[order[1]])
         mine[...] = mine[...] + second[0] + second[1] + second[2]
@@ -527,8 +529,9 @@
 
     def spread(self, g, s):
         _, inbox, _, third, done, _, recv = self.views(g, s)
-        order = ORDERS[s]
-        arrived(third, recv.at[4])
+        order = ORDERS[g][s]
+        if s == 0:
+            arrived(self.third.at[SLOTS[g]], self.third_recv.at[SLOTS[g]])
         part = rest(inbox.at[0], order, self.me[order[1]]).at[self.me[order[2]]]
         self.final[g, s] = part[...] + third[0] + third[1] + third[2]
         part = self.final.at[g, s]
@@ -538,8 +541,8 @@
         pltpu.make_async_copy(part, done.at[z], self.keep.at[g]).start()
 
     def finish(self, g, s):
-        third = self.views(g, s)[3]
-        arrived(third, self.spread_recv.at[g, s])
+        if s == 0:
+            arrived(self.third.at[SLOTS[g]], self.spread_recv.at[g])
 
     def sent(self, g):
         slot = SLOTS[g]
@@ -664,15 +667,17 @@
                  x_ref, act, slope, bufu, bufd, trigs, early_ref, late_ref, state, before, pay, after,
                  ratio_ref, inverse_ref, normal_ref, acc_ref, scale_ref, mixed_ref, normed_ref, gffn_ref, vec_ref, rows_ref,
                  bup, turned, stage, sums, first_in, second_in, third_in, final_ref, vecs,
-                 load_sem, core_send, core_recv, send, recv, keep_sem, spread_recv, spread_send, vec_send, vec_recv, free_sem, open_sem, *scratch):
+                 load_sem, core_send, core_recv, send, recv, keep_sem, spread_recv, spread_send, third_recv, vec_send, vec_recv, free_sem, open_sem, *scratch):
     everywhere = ("seq_0", "seq_1", "batch")
-    greet(everywhere)
     loads = {}
 
     def load(name, src, dst):
         copy = pltpu.make_async_copy(src, dst, load_sem.at[len(loads)])
         copy.start()
         loads[name] = copy
+
+    def load_shared(k, src, dst):
+        pltpu.make_async_copy(src, dst, load_sem.at[k]).start()
 
     def ready(*names):
         with jax.named_scope("ready"):
@@ -688,6 +693,7 @@
         load(f"wv{n}", wv_hbm.at[:, cols], bufd.at[2 * WIDTH : 3 * WIDTH, cols])
         load(f"wk{n}", wk_hbm.at[:, cols], bufd.at[WIDTH : 2 * WIDTH, cols])
     load("wq", wq_hbm, bufd.at[0:WIDTH])
+    greet(everywhere)
     for k, vector in enumerate((bq_in, bk_in, bv_in, bo_in, gain1_in, shift1_in, bdown_in, gain2_in, shift2_in)):
         load(f"row {k}", vector, rows_ref.at[k])
     load("bup", bup_in, bup.at[0])
@@ -715,20 +721,25 @@
         project_soft(n, x_ref, bufd.at[WIDTH : 2 * WIDTH], bk, trigs.at[1], act, HEADS, slope, 9)
         pl.when(n == 0)(lambda: greeted(everywhere))
         pl.when(n > 0)(lambda: earlier_sums.step(1, n - 1))
-        each_of(2, lambda j: state_sums(2 * n + j, act, slope, state, early_ref))
+        for j in range(2):
+            state_sums(2 * n + j, act, slope, state, early_ref)
         earlier_sums.step(0, n)
 
     def queries(n):
         project_soft(n, x_ref, bufd.at[0:WIDTH], bq, trigs.at[0], act, 0, slope, 6)
         pl.when(n == 0)(lambda: earlier_sums.step(1, 2))
 
-    def own(p):
-        pl.when(lax.rem(p, 2) == 0)(lambda: earlier_sums.step(2, p // 2))
-        attend_local(p, act, slope, ratio_ref, inverse_ref)
-
-    def earlier(p):
-        pl.when(lax.rem(p, 2) == 0)(lambda: earlier_sums.step(4, p // 2))
-        attend_earlier(p, act, early_ref, before, ratio_ref, inverse_ref, mixed_ref)
+    def own(n):
+        pl.when(n == 2)(lambda: earlier_sums.step(2, 2))
+        for j in range(2):
+            attend_local(2 * n + j, act, slope, ratio_ref, inverse_ref)
+        pl.when(n == 0)(lambda: earlier_sums.step(2, 1))
+
+    def earlier(n):
+        pl.when(n < 2)(lambda: earlier_sums.step(3, n + 1))
+        earlier_sums.step(4, n)
+        for j in range(2):
+            attend_earlier(2 * n + j, act, early_ref, before, ratio_ref, inverse_ref, mixed_ref)
 
     loop(3, keys, {n: lambda n=n: ready(f"wv{n + 1}", f"wk{n + 1}") for n in range(2)})
     ready("wq")
@@ -736,9 +747,10 @@
     load("wdown", wdown_hbm.at[0 : 3 * WIDTH], bufd.at[0 : 3 * WIDTH])
     load("qk_out", act, act_spill)
     load("v_out", slope, slope_spill)
-    loop(PAIRS, own)
-    each_of(3, lambda n: earlier_sums.step(3, n))
-    loop(PAIRS, earlier)
+    earlier_sums.step(2, 0)
+    loop(3, own)
+    earlier_sums.step(3, 0)
+    loop(3, earlier)
     ready("wo")
 
     def first_norm(r):
@@ -784,7 +796,7 @@
     loop(ROWS // CHUNK, second_norm)
     load("block", x_ref, block_out)
     red = Reduction(stage, sums, first_in, second_in, third_in, done_out, core_send, core_recv, send, recv, keep_sem,
-                    spread_recv, spread_send, final_ref)
+                    spread_recv, spread_send, third_recv, final_ref)
 
     def down_rows(y):
         turned[...] = act[:, at(y, WIDTH)].T
@@ -814,7 +826,7 @@
         for half in range(2):
             vec_ref[pl.ds(9 + 2 * t + half, 1), :] = total[:, WIDTH * half : WIDTH * half + WIDTH]
 
-    loads["wo again"] = pltpu.make_async_copy(wo_hbm, wo, load_sem.at[39])
+    loads["wo again"] = pltpu.make_async_copy(wo_hbm, wo, load_sem.at[34])
 
     def down_begun():
         red.each(red.begin, 0)
@@ -825,15 +837,12 @@
     red.each(red.begin, 1)
     ready("block")
     load("x again", x_hbm, x_ref)
-    load("wq again", wq_hbm, bufd.at[0:WIDTH])
-    load("wk again", wk_hbm, bufd.at[WIDTH : 2 * WIDTH])
-    load("wv again", wv_hbm, bufd.at[2 * WIDTH : 3 * WIDTH])
+    for k, w in enumerate((wq_hbm, wk_hbm, wv_hbm)):
+        load_shared(35, w, bufd.at[WIDTH * k : WIDTH * k + WIDTH])
     load("qk", act_spill, bufu.at[0:ROWS])
-    gates = []
     for i in range(2):
         for c in range(2):
-            gates.append(f"gate {i}{c}")
-            load(gates[-1], slope_spill.at[CHUNK * c : CHUNK * c + CHUNK, pl.ds(128 * HEADS + WIDTH * i, WIDTH)],
+            load_shared(36, slope_spill.at[CHUNK * c : CHUNK * c + CHUNK, pl.ds(128 * HEADS + WIDTH * i, WIDTH)],
                  bufu.at[ROWS:WIDTH, pl.ds(2 * WIDTH * i + WIDTH * c, WIDTH)])
     def up_columns(b):
         for n in range(3):
@@ -937,15 +946,13 @@
     each_of(3, lambda n: earlier_sums.step(5, n))
     ready("qk", "v")
 
-    def heads_sent(p):
-        heads_back(p)
-
-        @pl.when(lax.rem(p, 2) == 1)
-        def _():
-            later_sums.step(0, p // 2)
-            pl.when(p > 1)(lambda: later_sums.step(1, p // 2 - 1))
-
-    loop(PAIRS, heads_sent)
+    def heads_sent(n):
+        for j in range(2):
+            heads_back(2 * n + j)
+        later_sums.step(0, n)
+        pl.when(n > 0)(lambda: later_sums.step(1, n - 1))
+
+    loop(3, heads_sent)
     turned[...] = normed_ref[...].T
 
     def up_first():
@@ -956,7 +963,7 @@
     red.swaps(3)
     later_sums.step(2, 0)
     free(0)
-    ready(*gates)
+    arrived(bufu.at[ROWS:WIDTH], load_sem.at[36])
 
     def query_two(n):
         query_back(2 * n)
@@ -996,14 +1003,15 @@
 
     loop(3, own_two, {1: own_fourth})
     red.each(red.relay, 3)
-    each_of(3, lambda n: later_sums.step(3, n))
     red.each(red.spread, 0)
     release(0)
+    each_of(3, lambda n: later_sums.step(3, n))
     freed(1)
 
     def keys_values(n):
         later_sums.step(4, n)
-        each_of(2, lambda j: later(2 * n + j))
+        for j in range(2):
+            later(2 * n + j)
         each_of(2, lambda i: product(slope, 3 + 3 * i, 5, 2 * i, n))
 
     def keys_first():
@@ -1012,9 +1020,9 @@
         red.each(red.middle, 2)
 
     def keys_second():
+        red.each(red.follow, 4)
         red.each(red.spread, 1)
         release(1)
-        red.each(red.middle, 3)
 
     loop(3, keys_values, {0: keys_first, 1: keys_second})
     for i in range(3):
@@ -1025,28 +1033,28 @@
     red.each(red.begin, 5)
     vector_end(0)
     vector_start(1)
-    ready("wq again", "wk again", "wv again")
+    arrived(bufd.at[0 : 3 * WIDTH], load_sem.at[35])
 
     def back_first():
-        red.each(red.follow, 4)
         red.each(red.relay, 4)
+        red.each(red.middle, 3)
         red.each(red.last, 2)
 
     loop(ROWS // CHUNK, back, {0: back_first})
     load("tokens", acc_ref, tokens_out)
     red.each(red.relay, 5)
     red.each(red.follow, 5)
+    red.each(red.middle, 4)
     red.each(red.last, 3)
-    red.each(red.middle, 4)
-    red.each(red.spread, 2)
     vector_end(1)
     vector_start(2)
     red.each(red.middle, 5)
+    red.each(red.spread, 2)
     red.each(red.last, 4)
-    red.each(red.spread, 3)
     vector_end(2)
     vector_start(3)
     red.each(red.last, 5)
+    red.each(red.spread, 3)
     red.each(red.spread, 4)
     red.each(red.spread, 5)
     vector_end(3)
@@ -1108,9 +1116,9 @@
             ((1, HIDDEN), F32), ((WIDTH, ROWS), BF16),
             ((2, 3, 2, 4, 4, 4, 24, 128), F32), ((4, 3, 4, 4, 4, 24, 128), F32), ((4, 3, 3, 4, 4, 24, 128), F32),
             ((4, 3, 3, 4, 24, 128), F32), ((4, 3, 3, 24, 128), F32), ((6, 3, 24, 128), F32), ((11, 8, WIDTH), F32))]
-        + [pltpu.SemaphoreType.DMA((40,)), pltpu.SemaphoreType.DMA((4, 3)), pltpu.SemaphoreType.DMA((4, 3)),
-           pltpu.SemaphoreType.DMA((4, 3)), pltpu.SemaphoreType.DMA((4, 3, 5)), pltpu.SemaphoreType.DMA((6,)), pltpu.SemaphoreType.DMA((6, 3)),
-           pltpu.SemaphoreType.DMA((6,)),
+        + [pltpu.SemaphoreType.DMA((37,)), pltpu.SemaphoreType.DMA((4, 3)), pltpu.SemaphoreType.DMA((4, 3)),
+           pltpu.SemaphoreType.DMA((4, 3)), pltpu.SemaphoreType.DMA((4, 3, 4)), pltpu.SemaphoreType.DMA((6,)), pltpu.SemaphoreType.DMA((6,)),
+           pltpu.SemaphoreType.DMA((6,)), pltpu.SemaphoreType.DMA((4,)),
            pltpu.SemaphoreType.DMA((5,)), pltpu.SemaphoreType.DMA((5,)), pltpu.SemaphoreType.REGULAR((2,)), pltpu.SemaphoreType.REGULAR((2,))]
         + EXCHANGE_SCRATCH + QUARTER_SCRATCH,
         compiler_params=pltpu.CompilerParams(collective_id=1, has_side_effects=True, vmem_limit_bytes=LIMIT),

time: 120 us -> 118 us (0.983)
  Pallas kernels: 119 us -> 116 us
    pallas_call x1, Pallas kernels: 115 us -> 113 us  [on_device(): pl.pallas_call(layer_kernel, out_shape=[out(*shape) for shape in (wide16,...]
where the time goes in v2:
time: 118 us
  Pallas kernels  116 us (98%)
  between operations  1.47 us (1%)
    pallas_call x1, Pallas kernels, on_device(): pl.pallas_call(layer_kernel, out_shape=[out(*shape) for shape in (wide16,...  113 us
    pallas_call x1, Pallas kernels, on_device(): pl.pallas_call(final_kernel, out_shape=[out(*wide16), out(*wide32)] + [sq...  3.77 us

profile of v2, /device:TPU:0, one launch (start us, length us, event | category | flops | bytes accessed | tf_op | source)
XLA Modules:
  0.0 118.0 jit_solution(9701350348472127476)
XLA Ops:
  1.3 112.7 %shard_map.322 = (bf16[512,768]{1,0:T(8,128)(2,1)}, f32[512,768]{1,0:T(8,128)}, f32[6,3,4,24,128]{4,3,2,1,0:T(8,128)}, f32[16,768]{1,0:T(8,128)}, bf16[512,3072]{1,0:T(8,128)(2,1)}, /*index=5*/bf16[512,3072]{1,0:T(8,128)(2,1)}) custom-call(s32[1]{0:T(128)S(6)} %copy.37.len_ref, f32[768]{0:T(1024)} %bq_in.1, f32[768]{0:T(1024)} %bk_in.1, f32[768]{0:T(1024)} %bv_in.1, ...), custom_call_target="tpu_custom_call" | custom-call | tf_op jit(solution)/shard_map/pallas_call | solution.py:1107
  114.0 3.8 %shard_map.323 = (bf16[512,768]{1,0:T(8,128)(2,1)}, f32[512,768]{1,0:T(8,128)}, f32[24,768]{1,0:T(8,128)}, f32[24]{0:T(128)}, f32[24,768]{1,0:T(8,128)}, /*index...) custom-call(f32[6,3,4,24,128]{4,3,2,1,0:T(8,128)} %get-tuple-element, ...), custom_call_target="tpu_custom_call" | custom-call | tf_op jit(solution)/shard_map/pallas_call | solution.py:1128

commit v3 on v2

--- a/solution.py
+++ b/solution.py
@@ -836,14 +836,15 @@
     red.each(red.follow, 0)
     red.each(red.begin, 1)
     ready("block")
-    load("x again", x_hbm, x_ref)
-    for k, w in enumerate((wq_hbm, wk_hbm, wv_hbm)):
-        load_shared(35, w, bufd.at[WIDTH * k : WIDTH * k + WIDTH])
     load("qk", act_spill, bufu.at[0:ROWS])
     for i in range(2):
         for c in range(2):
             load_shared(36, slope_spill.at[CHUNK * c : CHUNK * c + CHUNK, pl.ds(128 * HEADS + WIDTH * i, WIDTH)],
                  bufu.at[ROWS:WIDTH, pl.ds(2 * WIDTH * i + WIDTH * c, WIDTH)])
+    load("x again", x_hbm, x_ref)
+    for k, w in enumerate((wq_hbm, wk_hbm, wv_hbm)):
+        load_shared(35, w, bufd.at[WIDTH * k : WIDTH * k + WIDTH])
+
     def up_columns(b):
         for n in range(3):
             cols = pl.ds(pl.multiple_of(WIDTH * b + 256 * n, 256), 256)
@@ -961,7 +962,6 @@
 
     loop(4, up_columns, {0: up_first, 2: lambda: red.each(red.middle, 0)})
     red.swaps(3)
-    later_sums.step(2, 0)
     free(0)
     arrived(bufu.at[ROWS:WIDTH], load_sem.at[36])
 
@@ -970,17 +970,18 @@
         query_back(2 * n + 1)
 
     def query_second():
+        later_sums.step(2, 0)
         later_sums.step(2, 1)
         red.each(red.begin, 2)
 
     def query_fourth():
         later_sums.step(2, 2)
-        later_sums.step(6, 0)
         red.each(red.middle, 1)
 
     loop(3, query_two, {0: query_second, 1: query_fourth})
     red.each(red.begin, 3)
     red.each(red.follow, 2)
+    later_sums.step(6, 0)
     later_sums.step(6, 1)
     red.each(red.last, 0)
     free(1)

time: 118 us -> 118 us (level)
  no operation moved by 1% of the time
where the time goes in v3:
time: 118 us
  Pallas kernels  117 us (99%)
  between operations  1.47 us (1%)
    pallas_call x1, Pallas kernels, on_device(): pl.pallas_call(layer_kernel, out_shape=[out(*shape) for shape in (wide16,...  113 us
    pallas_call x1, Pallas kernels, on_device(): pl.pallas_call(final_kernel, out_shape=[out(*wide16), out(*wide32)] + [sq...  3.77 us

profile of v3, /device:TPU:0, one launch (start us, length us, event | category | flops | bytes accessed | tf_op | source)
XLA Modules:
  0.0 118.0 jit_solution(1789376962035240186)
XLA Ops:
  1.3 112.7 %shard_map.322 = (bf16[512,768]{1,0:T(8,128)(2,1)}, f32[512,768]{1,0:T(8,128)}, f32[6,3,4,24,128]{4,3,2,1,0:T(8,128)}, f32[16,768]{1,0:T(8,128)}, bf16[512,3072]{1,0:T(8,128)(2,1)}, /*index=5*/bf16[512,3072]{1,0:T(8,128)(2,1)}) custom-call(s32[1]{0:T(128)S(6)} %copy.37.len_ref, f32[768]{0:T(1024)} %bq_in.1, f32[768]{0:T(1024)} %bk_in.1, f32[768]{0:T(1024)} %bv_in.1, ...), custom_call_target="tpu_custom_call" | custom-call | tf_op jit(solution)/shard_map/pallas_call | solution.py:1108
  114.1 3.8 %shard_map.323 = (bf16[512,768]{1,0:T(8,128)(2,1)}, f32[512,768]{1,0:T(8,128)}, f32[24,768]{1,0:T(8,128)}, f32[24]{0:T(128)}, f32[24,768]{1,0:T(8,128)}, /*index...) custom-call(f32[6,3,4,24,128]{4,3,2,1,0:T(8,128)} %get-tuple-element, ...), custom_call_target="tpu_custom_call" | custom-call | tf_op jit(solution)/shard_map/pallas_call | solution.py:1129
